TPU v7x, 256 devices: a whole 4x4x8 slice. The times are simulated.
256 devices in a mesh: seq: 128 (over x, z_hi, y, core), head: 2 (over z_lo).
Axes of the slice: x: 4, y: 4, z: 8 (z_hi: 4, z_lo: 2; z = z_hi * 2 + z_lo), core: 2. Of those that a mesh axis runs over, the one named last changes fastest.
Arguments:
- cur_query: bfloat16 [16384, 1536], P('seq', 'head'), may hold values from -6 to 6
- cur_key: bfloat16 [16384, 1536], P('seq', 'head'), may hold values from -6 to 6
- cur_value: bfloat16 [16384, 1536], P('seq', 'head'), may hold values from -6 to 6
- grad_out: bfloat16 [16384, 1536], P('seq', 'head'), may hold values from -6 to 6
- out_weight: bfloat16 [1536, 1536], P(None, 'head'), may hold values from -0.15625 to 0.15625
- half_key: bfloat16 [3840, 1536], P('seq', 'head'), may hold values from -6 to 6
- half_value: bfloat16 [3840, 1536], P('seq', 'head'), may hold values from -6 to 6
- quart_key: bfloat16 [1024, 1536], P('seq', 'head'), may hold values from -6 to 6
- quart_value: bfloat16 [1024, 1536], P('seq', 'head'), may hold values from -6 to 6
- cur_count: int32 [16, 8], replicated, may hold values from 1 to 128, 960 in all within a row
- section_bias: float32 [2, 24], P(None, 'head'), may hold values from -1 to 1
Outputs:
- d_query: bfloat16 [16384, 1536], P('seq', 'head')
- d_key: bfloat16 [16384, 1536], P('seq', 'head')
- d_value: bfloat16 [16384, 1536], P('seq', 'head')
- d_half_key: bfloat16 [3840, 1536], P('seq', 'head')
- d_half_value: bfloat16 [3840, 1536], P('seq', 'head')
- d_quart_key: bfloat16 [1024, 1536], P('seq', 'head')
- d_quart_value: bfloat16 [1024, 1536], P('seq', 'head')
- d_section_bias: float32 [2, 24], P(None, 'head')
Inputs may be any that keep to these rules, and one draw needn't show every extreme that they name: The first cur_count[c, s] slots of shard s of clip c hold real tokens, the rest padding; every row sums to 960 and its largest entry is 128.
All inputs are finite; a program needn't handle non-finite values.
Results may differ from a plain program's by a relative error of at most 0.025.
Values may be sent and summed in bfloat16 or wider, within the bound.
A program may use at most 128 MiB of HBM per device.

v0:
```python
import jax
import jax.numpy as jnp
import numpy as np
from jax import lax
from jax.sharding import PartitionSpec as P

HD = 64
GROUP = 8


def partner_2(value, axis, stride):
    mask = 2**stride
    pairs = [(source, source ^ mask) for source in range(lax.axis_size(axis))]
    return lax.ppermute(value, axis, pairs)


def shards(
    cur_query,
    cur_key,
    cur_value,
    grad_out,
    out_weight,
    half_key,
    half_value,
    quart_key,
    quart_value,
    cur_count,
    section_bias,
):
    token_rows = cur_query.shape[0]
    feature_width = cur_query.shape[1]
    half_rows = half_key.shape[0]
    quart_rows = quart_key.shape[0]
    block_rows = token_rows + half_rows + quart_rows
    heads_here = feature_width // HD
    score_scale = HD ** (-0.5)
    seq_index = lax.axis_index("seq")
    member = seq_index % GROUP
    clip_index = seq_index // GROUP
    group_counts = lax.dynamic_slice_in_dim(cur_count, clip_index, 1, 0)[0]
    member_ids = jnp.arange(GROUP, dtype=jnp.int32)
    own_count = jnp.sum(jnp.where(member_ids == member, group_counts, 0))
    valid_row = jnp.arange(token_rows, dtype=jnp.int32) < own_count
    cotangent = lax.all_gather(grad_out, "head", axis=1, tiled=True)
    cotangent = jnp.where(valid_row[:, None], cotangent, jnp.zeros_like(cotangent))
    adjoint = jnp.dot(cotangent, out_weight, preferred_element_type=jnp.float32).astype(
        jnp.bfloat16
    )
    own_block = jnp.stack(
        [
            jnp.concatenate([cur_key, half_key, quart_key], axis=0),
            jnp.concatenate([cur_value, half_value, quart_value], axis=0),
        ]
    )
    bit_total = GROUP.bit_length() - 1
    gather_bits = list(range(bit_total))
    layout = [0]
    gathered = own_block
    for bit_number in gather_bits:
        partner = partner_2(gathered, "seq", bit_number)
        upper_bit = member >> bit_number & 1
        gathered = jnp.where(
            upper_bit == 1,
            jnp.concatenate([partner, gathered], axis=1),
            jnp.concatenate([gathered, partner], axis=1),
        )
        layout = layout + [entry + (1 << bit_number) for entry in layout]
    slot_kind = np.concatenate(
        [
            np.zeros(token_rows, np.int32),
            np.ones(half_rows, np.int32),
            np.full(quart_rows, 2, np.int32),
        ]
    )
    kind_onehot = jnp.asarray((slot_kind[:, None] == np.arange(3)[None, :]).astype(np.float32))
    bias_table = jnp.concatenate([jnp.zeros((1, heads_here), jnp.float32), section_bias], axis=0)
    block_bias = jnp.dot(kind_onehot, bias_table, precision=lax.Precision.HIGHEST)
    key_bias = jnp.tile(block_bias, (GROUP, 1)).T
    section_table = jnp.tile(kind_onehot[:, 1:], (GROUP, 1))
    counts_layout = group_counts[np.array(layout, np.int32)]
    slot_ids = jnp.arange(block_rows, dtype=jnp.int32)
    key_valid = (
        (slot_ids[None, :] >= token_rows) | (slot_ids[None, :] < counts_layout[:, None])
    ).reshape(-1)
    all_keys = gathered[0]
    all_values = gathered[1]
    pair_size = 2
    pair_width = pair_size * HD
    query_parts = []
    key_parts = []
    value_parts = []
    bias_parts = []
    for pair_index in range(heads_here // pair_size):
        first_col = pair_index * pair_width
        query_pair = cur_query[:, first_col : first_col + pair_width].reshape(
            token_rows, pair_size, HD
        )
        key_pair = all_keys[:, first_col : first_col + pair_width].reshape(-1, pair_size, HD)
        value_pair = all_values[:, first_col : first_col + pair_width].reshape(-1, pair_size, HD)
        adjoint_pair = adjoint[:, first_col : first_col + pair_width].reshape(
            token_rows, pair_size, HD
        )
        bias_pair = key_bias[pair_index * pair_size : (pair_index + 1) * pair_size]
        scores = (
            jnp.einsum("qhd,khd->hqk", query_pair, key_pair, preferred_element_type=jnp.float32)
            * score_scale
        )
        scores = scores + bias_pair[:, None, :]
        scores = jnp.where(key_valid[None, None, :], scores, jnp.float32(-1e30))
        row_top = jnp.max(scores, axis=2, keepdims=True)
        exponent = jnp.exp(scores - row_top)
        softmax_probs = exponent / jnp.sum(exponent, axis=2, keepdims=True)
        probs_low = softmax_probs.astype(jnp.bfloat16)
        attn_pair = jnp.einsum(
            "hqk,khd->qhd", probs_low, value_pair, preferred_element_type=jnp.float32
        ).astype(jnp.bfloat16)
        d_prob = jnp.einsum(
            "qhd,khd->hqk", adjoint_pair, value_pair, preferred_element_type=jnp.float32
        )
        row_delta = jnp.sum(
            adjoint_pair.astype(jnp.float32) * attn_pair.astype(jnp.float32), axis=2
        ).T[:, :, None]
        d_score = softmax_probs * (d_prob - row_delta)
        score_low = d_score.astype(jnp.bfloat16)
        query_grad = (
            jnp.einsum("hqk,khd->qhd", score_low, key_pair, preferred_element_type=jnp.float32)
            * score_scale
        )
        query_parts.append(query_grad.astype(jnp.bfloat16).reshape(token_rows, pair_width))
        key_grad = (
            jnp.einsum("hqk,qhd->khd", score_low, query_pair, preferred_element_type=jnp.float32)
            * score_scale
        )
        key_parts.append(key_grad.astype(jnp.bfloat16).reshape(-1, pair_width))
        value_grad = jnp.einsum(
            "hqk,qhd->khd", probs_low, adjoint_pair, preferred_element_type=jnp.float32
        )
        value_parts.append(value_grad.astype(jnp.bfloat16).reshape(-1, pair_width))
        key_sums = jnp.sum(d_score, axis=1)
        bias_parts.append(jnp.dot(key_sums, section_table, precision=lax.Precision.HIGHEST))
    d_query = jnp.concatenate(query_parts, axis=1)
    bias_term = jnp.concatenate(bias_parts, axis=0).T
    d_section_bias = lax.psum(bias_term, "seq")
    summed = jnp.stack(
        [jnp.concatenate(key_parts, axis=1), jnp.concatenate(value_parts, axis=1)]
    ).astype(jnp.float32)
    for bit_number in gather_bits[::-1]:
        half_length = summed.shape[1] // 2
        lower_half = summed[:, :half_length]
        upper_half = summed[:, half_length:]
        upper_bit = member >> bit_number & 1
        kept_half = jnp.where(upper_bit == 1, upper_half, lower_half)
        sent_half = jnp.where(upper_bit == 1, lower_half, upper_half).astype(jnp.bfloat16)
        arrived = partner_2(sent_half, "seq", bit_number)
        summed = kept_half + arrived.astype(jnp.float32)
    result = summed.astype(jnp.bfloat16)
    d_key = result[0, :token_rows]
    d_value = result[1, :token_rows]
    d_half_key = result[0, token_rows : token_rows + half_rows]
    d_half_value = result[1, token_rows : token_rows + half_rows]
    d_quart_key = result[0, token_rows + half_rows :]
    d_quart_value = result[1, token_rows + half_rows :]
    return (
        d_query,
        d_key,
        d_value,
        d_half_key,
        d_half_value,
        d_quart_key,
        d_quart_value,
        d_section_bias,
    )


def solution(mesh):
    return jax.shard_map(
        shards,
        mesh=mesh,
        in_specs=(
            P("seq", "head"),
            P("seq", "head"),
            P("seq", "head"),
            P("seq", "head"),
            P(None, "head"),
            P("seq", "head"),
            P("seq", "head"),
            P("seq", "head"),
            P("seq", "head"),
            P(),
            P(None, "head"),
        ),
        out_specs=(
            P("seq", "head"),
            P("seq", "head"),
            P("seq", "head"),
            P("seq", "head"),
            P("seq", "head"),
            P("seq", "head"),
            P("seq", "head"),
            P(None, "head"),
        ),
        check_vma=False,
    )
```

profile of v0, /device:TPU:1, one launch (start us, length us, event | category | flops | bytes accessed | tf_op | source)
XLA Modules:
  0.0 656.1 jit_solution(7899341449832215882)
XLA Ops:
  2.7 3.3 collective-permute-start
  11.5 24.1 %collective-permute-done.1 = bf16[2,332,768]{2,0,1:T(2,128)(2,1)} collective-permute-done((bf16[2,332,768]{2,0,1:T(2,128)(2,1)}, bf16[2,332,768]{2,0,1:T(2,128)(2,1)}, u32[]{:S(2)}, u32[]{:S(2)}) %collective-permute-start.1) | collective-permute-done | bytes 1019936 | tf_op jit(solution)/shard_map/ppermute | solution.py:14
  36.9 2.1 maximum_select_fusion.1
  45.1 6.0 all_gather.3
  54.4 31.2 %collective-permute-done.2 = bf16[2,664,768]{2,1,0:T(8,128)(2,1)} collective-permute-done((bf16[2,664,768]{2,1,0:T(8,128)(2,1)}, bf16[2,664,768]{2,1,0:T(8,128)(2,1)}, u32[]{:S(2)}, u32[]{:S(2)}) %collective-permute-start.2) | collective-permute-done | bytes 2039840 | tf_op jit(solution)/shard_map/ppermute | solution.py:14
  85.6 4.9 maximum_select_fusion
  106.5 2.1 fusion.131
  113.4 2.6 fusion.137
  117.3 2.1 fusion.132
  129.2 2.1 fusion.133
  136.1 2.6 fusion.139
  141.7 2.3 fusion.134
  150.3 2.1 fusion.135
  158.7 2.1 fusion.136
  169.1 22.6 %copy.253 = bf16[1,1328,768]{2,0,1:T(2,128)(2,1)S(1)} copy(bf16[1,1328,768]{2,1,0:T(8,128)(2,1)S(1)} %bitcast.289) | data formatting | bytes 4079616 | tf_op jit(solution)/shard_map/stack | solution.py:144
  193.0 22.6 %copy.252 = bf16[1,1328,768]{2,0,1:T(2,128)(2,1)S(1)} copy(bf16[1,1328,768]{2,1,0:T(8,128)(2,1)S(1)} %bitcast.288) | data formatting | bytes 4079616 | tf_op jit(solution)/shard_map/stack | solution.py:144
  215.6 9.8 %maximum_convert_fusion = f32[2,1328,768]{2,0,1:T(2,128)S(1)} fusion(bf16[1,1328,768]{2,0,1:T(2,128)(2,1)S(1)} %copy.253, bf16[1,1328,768]{2,0,1:T(2,128)(2,1)S(1)} %copy.252), kind=kLoop, calls=%fused_computation.8 | loop fusion | flops 8159232 | bytes 12238848 | tf_op jit(solution)/shard_map/convert_element_type | solution.py:146
  225.4 3.1 copy-done.2
  228.6 3.4 select_convert_fusion
  236.6 40.9 %collective-permute-done.3 = bf16[2,664,768]{2,0,1:T(2,128)(2,1)} collective-permute-done((bf16[2,664,768]{2,0,1:T(2,128)(2,1)}, bf16[2,664,768]{2,0,1:T(2,128)(2,1)}, u32[]{:S(2)}, u32[]{:S(2)}) %collective-permute-start.3) | collective-permute-done | bytes 2039840 | tf_op jit(solution)/shard_map/ppermute | solution.py:14
  277.6 5.7 convert_add_fusion
  289.3 351.4 %psum.7 = f32[2,12]{1,0:T(2,128)} all-reduce(f32[2,12]{1,0:T(2,128)S(1)} %bitcast.369), channel_id=1, replica_groups=mesh['seq'=128,'head'=2] {'seq'}, use_global_device_ids=true, to_apply=%region_25.26 | all-reduce | flops 24 | bytes 192 | tf_op jit(solution)/shard_map/psum | solution.py:143
  640.7 3.0 convert_add_fusion.1
  644.3 4.7 collective-permute-start.5
  (259 shorter events, 97.2 us)
Async XLA Ops:
  0.6 51.8 %copy-start = (bf16[1536,768]{1,0:T(8,128)(2,1)S(1)}, bf16[1536,768]{1,0:T(8,128)(2,1)}, u32[]{:S(2)}) copy-start(bf16[1536,768]{1,0:T(8,128)(2,1)} %param.18) | copy-start | bytes 7077892
  2.7 5.0 collective-permute-start
  11.5 24.1 %collective-permute-start.1 = (bf16[2,332,768]{2,0,1:T(2,128)(2,1)}, bf16[2,332,768]{2,0,1:T(2,128)(2,1)}, u32[]{:S(2)}, u32[]{:S(2)}) collective-permute-start(bf16[2,332,768]{2,0,1:T(2,128)(2,1)} %copy.207), channel_id=1, source_target_pairs={{0,4},{2,6},{4,0},{6,2},{8,12},{10,14},{12,8},{14,10},{16,20},{18,... | collective-permute-start | bytes 3059720 | tf_op jit(solution)/shard_map/ppermute | solution.py:14
  36.9 4.4 copy-start.49
  36.9 4.4 copy-start.54
  39.1 6.0 copy-start.45
  39.1 46.5 %collective-permute-start.2 = (bf16[2,664,768]{2,1,0:T(8,128)(2,1)}, bf16[2,664,768]{2,1,0:T(8,128)(2,1)}, u32[]{:S(2)}, u32[]{:S(2)}) collective-permute-start(bf16[2,664,768]{2,1,0:T(8,128)(2,1)} %maximum_select_fusion.1), channel_id=1, source_target_pairs={{0,8},{2,10},{4,12},{6,14},{8,0},{10,2},{12,4},{14,6},{16,24},{18,... | collective-permute-start | bytes 6119432 | tf_op jit(solution)/shard_map/ppermute | solution.py:14
  100.8 4.3 copy-start.43
  100.8 5.2 copy-start.42
  102.0 56.7 %copy-start.19 = (bf16[1328,128]{0,1:T(8,128)(2,1)}, bf16[1328,128]{0,1:T(8,128)(2,1)S(1)}, u32[]{:S(2)}) copy-start(bf16[1328,128]{0,1:T(8,128)(2,1)S(1)} %copy.230) | copy-start | bytes 1019908
  102.1 4.2 copy-start.41
  106.2 11.1 %copy-start.26 = (bf16[1328,128]{0,1:T(8,128)(2,1)}, bf16[1328,128]{0,1:T(8,128)(2,1)S(1)}, u32[]{:S(2)}) copy-start(bf16[1328,128]{0,1:T(8,128)(2,1)S(1)} %copy.214) | copy-start | bytes 1019908
  126.2 5.1 copy-start.4
  138.7 5.3 copy-start.6
  169.1 22.6 %copy-start.31 = (bf16[1328,128]{1,0:T(8,128)(2,1)S(1)}, bf16[1328,128]{1,0:T(8,128)(2,1)}, u32[]{:S(2)}) copy-start(bf16[1328,128]{1,0:T(8,128)(2,1)} %copy.241) | copy-start | bytes 1019908
  169.1 22.7 %copy-start.33 = (bf16[1328,128]{1,0:T(8,128)(2,1)S(1)}, bf16[1328,128]{1,0:T(8,128)(2,1)}, u32[]{:S(2)}) copy-start(bf16[1328,128]{1,0:T(8,128)(2,1)} %copy.242) | copy-start | bytes 1019908
  228.6 4.6 copy-start.53
  228.6 4.7 copy-start.56
  228.6 6.2 copy-start.5
  228.6 6.2 copy-start.27
  232.0 45.6 %collective-permute-start.3 = (bf16[2,664,768]{2,0,1:T(2,128)(2,1)}, bf16[2,664,768]{2,0,1:T(2,128)(2,1)}, u32[]{:S(2)}, u32[]{:S(2)}) collective-permute-start(bf16[2,664,768]{2,0,1:T(2,128)(2,1)} %select_convert_fusion), channel_id=1, source_target_pairs={{0,8},{2,10},{4,12},{6,14},{8,0},{10,2},{12,4},{14,6},{16,24},{18,... | collective-permute-start | bytes 6119432 | tf_op jit(solution)/shard_map/ppermute | solution.py:14
  286.3 354.4 %collective-permute-start.4 = (bf16[2,332,768]{2,0,1:T(2,128)(2,1)S(1)}, bf16[2,332,768]{2,0,1:T(2,128)(2,1)S(1)}, u32[]{:S(2)}, u32[]{:S(2)}) collective-permute-start(bf16[2,332,768]{2,0,1:T(2,128)(2,1)S(1)} %select_convert_fusion.1), channel_id=1, source_target_pairs={{0,4},{2,6},{4,0},{6,2},{8,12},{10,14},{12,8},{14,10},{16,20},{18,... | collective-permute-start | bytes 3059720 | tf_op jit(solution)/shard_map/ppermute | solution.py:14
  644.3 6.2 collective-permute-start.5
  651.3 4.6 copy-start.1
  (39 other events, 79.0 us)
where the time goes:
time: 662 us; the launch traced here: 656 us
  blocking collectives  357 us (54%)
  local copies, waits for them, and re-layouts  101 us (15%)
  waiting for transfers between devices  99.3 us (15%)
  other arithmetic  44.9 us (7%)
  matrix products  40.3 us (6%)
  starting transfers between devices  11.4 us (2%)
    psum x1, blocking collectives, shards(): d_section_bias = lax.psum(bias_term, 'seq')  351 us
    ppermute x6, waiting for transfers between devices, partner_2(): return lax.ppermute(value, axis, pairs)  99.3 us
    another operation x2, local copies, waits for them, and re-layouts, shards(): jnp.stack([jnp.concatenate(key_parts, axis=1), jnp.concatenate(value_part...  45.2 us
    dot_general x6, matrix products, shards(): jnp.einsum('qhd,khd->hqk', adjoint_pair, value_pair, preferred_element_ty...  13.4 us
  transfers between devices with their start and end apart: 6, of which 5 were waited for; matrix products, arithmetic and copies ran while one was open for 2% of the time, Pallas kernels for 0%

commit v1 on v0

v1 whole, which is shorter than its diff:
```python
import functools

import jax
import jax.numpy as jnp
from jax import lax
from jax.experimental import pallas as pl
from jax.experimental.pallas import tpu as pltpu
from jax.sharding import PartitionSpec as P

HD = 64
LANES = 128
CHIPS = 4
HEADS = 3
MESH = pl.DeviceIdType.MESH
BF = jnp.bfloat16
F32 = jnp.float32


def dot(a, b, ca, cb):
    return lax.dot_general(a, b, (((ca,), (cb,)), ((), ())), preferred_element_type=F32)


def joined(a, b, upper):
    if upper:
        return jnp.concatenate([a[:, HD:], b[:, HD:]], axis=1)
    return jnp.concatenate([a[:, :HD], b[:, :HD]], axis=1)


def exchange_kernel(
    n_x,
    n_z,
    query_hbm,
    key_hbm,
    value_hbm,
    grad_hbm,
    weight_hbm,
    half_key,
    half_value,
    quart_key,
    quart_value,
    counts,
    section_bias,
    dq_out,
    dkv_out,
    bias_out,
    query,
    key,
    value,
    grad,
    grad_far,
    weight,
    kv_send,
    qa_send,
    kv_all,
    qa_all,
    count_bias,
    key_bias,
    scores,
    d_probs,
    low,
    part_send,
    part_got,
    own_sum,
    dkv_send,
    dq_send,
    bias_send,
    bias_clip,
    bias_x,
    bias_z,
    load_sem,
    z_sem,
    kv_ss,
    kv_rs,
    sib_ss,
    sib_rs,
    fwd_ss,
    fwd_rs,
    qa_ss,
    qa_rs,
    part_ss,
    part_rs,
    dkv_ss,
    dkv_rs,
    dq_ss,
    dq_rs,
    clip_ss,
    clip_rs,
    x_ss,
    x_rs,
    zz_ss,
    zz_rs,
):
    rows = query_hbm.shape[0]
    half_rows = half_key.shape[0]
    quart_rows = quart_key.shape[0]
    width = query_hbm.shape[1]
    block = kv_send.shape[1]
    quart_at = block - 16
    heads = width // HD
    seq = lax.axis_index("seq")
    head = lax.axis_index("head")
    core = seq % 2
    y = seq // 2 % CHIPS
    z = seq // 8 % n_z
    x = seq // (8 * n_z)
    clip = seq // 8

    def device(x, z, y, core):
        return ((x * n_z + z) * CHIPS + y) * 2 + core

    def chip(dy):
        return (y + dy) % CHIPS

    def copy(src, dst, ss, rs, seq_to, head_to=None):
        return pltpu.make_async_remote_copy(
            src_ref=src,
            dst_ref=dst,
            send_sem=ss,
            recv_sem=rs,
            device_id={"seq": seq_to, "head": head if head_to is None else head_to},
            device_id_type=MESH,
        )

    loads = [
        pltpu.make_async_copy(a, b, load_sem.at[i])
        for i, (a, b) in enumerate(
            [
                (key_hbm, key),
                (value_hbm, value),
                (grad_hbm, grad),
                (query_hbm, query),
                (weight_hbm, weight),
            ]
        )
    ]
    for load in loads:
        load.start()

    sibling = device(x, z, y, 1 - core)
    partners = [(device(x, z, chip(dy), c), head) for dy in range(CHIPS) for c in (core, 1 - core)][1:]
    partners += [(device((x + d) % n_x, z, y, core), head) for d in range(1, n_x)]
    partners += [(device(x, (z + d) % n_z, y, core), head) for d in range(1, n_z)]
    partners += [(seq, 1 - head)]
    barrier = pltpu.get_barrier_semaphore()
    for seq_to, head_to in partners:
        pl.semaphore_signal(
            barrier, inc=1, device_id={"seq": seq_to, "head": head_to}, device_id_type=MESH
        )

    loads[0].wait()
    loads[1].wait()
    zeros = jnp.zeros((block - rows, LANES), BF)
    for i in range(heads // 2):
        cols = slice(i * LANES, (i + 1) * LANES)
        for upper in (False, True):
            at = 2 * i + upper
            kv_send[at, :rows] = joined(key[:, cols], value[:, cols], upper)
            kv_send[at, rows:] = zeros
            kv_send[at, rows : rows + half_rows] = joined(
                half_key[:, cols], half_value[:, cols], upper
            )
            kv_send[at, quart_at : quart_at + quart_rows] = joined(
                quart_key[:, cols], quart_value[:, cols], upper
            )

    pl.semaphore_wait(barrier, len(partners))

    z_copy = copy(grad_hbm, grad_far, z_sem.at[0], z_sem.at[1], seq, 1 - head)
    z_copy.start()
    kv_copies = {}
    sib_copies = []
    for j in range(HEADS):
        for dy in (1, 3, 2):
            c = copy(
                kv_send.at[HEADS * chip(dy) + j],
                kv_all.at[j, 0, dy],
                kv_ss.at[j, dy],
                kv_rs.at[j, dy],
                device(x, z, chip(dy), core),
            )
            c.start()
            kv_copies[j, dy] = c
        c = copy(
            kv_send.at[HEADS * y + j], kv_all.at[j, 1, 0], sib_ss.at[j], sib_rs.at[j], sibling
        )
        c.start()
        sib_copies.append(c)
        kv_all[j, 0, 0] = kv_send[HEADS * y + j]

    row_id = lax.broadcasted_iota(jnp.int32, (rows, LANES), 0)
    for c in range(2 * CHIPS):
        p, dy = divmod(c, CHIPS)
        shard = 2 * chip(CHIPS - dy) + (core if p == 0 else 1 - core)
        count_bias[c] = jnp.where(row_id < counts[clip, shard], F32(0), F32(-1e30))

    loads[2].wait()
    loads[4].wait()
    adjoint = dot(grad[...], weight[pl.ds(pl.multiple_of(head * width, LANES), width), :], 1, 0)

    fwd_copies = {}

    def forward(j):
        for dy in (1, 3, 2):
            kv_copies[j, dy].wait_recv()
            c = copy(
                kv_all.at[j, 0, dy],
                kv_all.at[j, 1, dy],
                fwd_ss.at[j, dy],
                fwd_rs.at[j, dy],
                sibling,
            )
            c.start()
            fwd_copies[j, dy] = c

    forward(0)
    forward(1)
    loads[3].wait()
    z_copy.wait()
    adjoint += dot(
        grad_far[...], weight[pl.ds(pl.multiple_of((1 - head) * width, LANES), width), :], 1, 0
    )
    own_count = counts[clip, 2 * y + core]
    row_wide = lax.broadcasted_iota(jnp.int32, (rows, width), 0)
    adjoint = jnp.where(row_wide < own_count, adjoint, F32(0)).astype(BF)
    for i in range(heads // 2):
        cols = slice(i * LANES, (i + 1) * LANES)
        scaled = query[:, cols] * BF(HD**-0.5)
        for upper in (False, True):
            qa_send[2 * i + upper] = joined(scaled, adjoint[:, cols], upper)
    qa_copies = {}
    for j in range(HEADS):
        for dy in (1, 3, 2):
            c = copy(
                qa_send.at[HEADS * chip(dy) + j],
                qa_all.at[j, dy],
                qa_ss.at[j, dy],
                qa_rs.at[j, dy],
                device(x, z, chip(dy), core),
            )
            c.start()
            qa_copies[j, dy] = c
        qa_all[j, 0] = qa_send[HEADS * y + j]
    forward(2)

    bias_row = lax.broadcasted_iota(jnp.int32, (8, LANES), 0)
    bias_lane = lax.broadcasted_iota(jnp.int32, (8, LANES), 1)
    hist_id = lax.broadcasted_iota(jnp.int32, (block - rows, LANES), 0)
    queries = CHIPS * rows
    groups = queries // LANES
    lane_id = lax.broadcasted_iota(jnp.int32, (queries, LANES), 1)

    def fold(t, op):
        total = t[:8]
        for r in range(8, t.shape[0], 8):
            total = op(total, t[r : r + 8])
        return total

    bias_total = jnp.zeros((8, LANES), F32)
    out_copies = []
    for j in range(HEADS):
        for dy in (1, 3, 2):
            qa_copies[j, dy].wait_recv()
            fwd_copies[j, dy].wait_recv()
        sib_copies[j].wait_recv()
        my_head = HEADS * y + j
        half_bias = section_bias[0, my_head]
        quart_bias = section_bias[1, my_head]
        hist_bias = jnp.where(
            hist_id < half_rows,
            half_bias,
            jnp.where(
                (hist_id >= quart_at - rows) & (hist_id < quart_at - rows + quart_rows),
                quart_bias,
                F32(-1e30),
            ),
        )
        qa = qa_all[j].reshape(queries, LANES)
        q_part = jnp.where(lane_id < HD, qa, BF(0))
        a_part = jnp.where(lane_id < HD, BF(0), qa)
        top = jnp.full((8, queries), -3e38, F32)
        for c in range(2 * CHIPS):
            s = dot(kv_all[j, c // CHIPS, c % CHIPS], q_part, 1, 1)
            bias = jnp.concatenate([count_bias[c], hist_bias], axis=0)
            s = s + jnp.concatenate([bias] * groups, axis=1)
            scores[c] = s
            top = jnp.maximum(top, fold(s, jnp.maximum))
        top = jnp.max(top, axis=0, keepdims=True)
        total = jnp.zeros((8, queries), F32)
        delta = jnp.zeros((8, queries), F32)
        for c in range(2 * CHIPS):
            dp = dot(kv_all[j, c // CHIPS, c % CHIPS], a_part, 1, 1)
            e = jnp.exp(scores[c] - top)
            scores[c] = e
            d_probs[c] = dp
            total = total + fold(e, jnp.add)
            delta = delta + fold(e * dp, jnp.add)
        inverse = 1.0 / jnp.sum(total, axis=0, keepdims=True)
        delta = jnp.sum(delta, axis=0, keepdims=True) * inverse
        both = jnp.concatenate([q_part, a_part], axis=0)
        half_sum = jnp.zeros((8, queries), F32)
        quart_sum = jnp.zeros((8, queries), F32)
        for c in list(range(CHIPS, 2 * CHIPS)) + list(range(CHIPS)):
            probs = scores[c] * inverse
            ds = probs * (d_probs[c] - delta)
            half_sum = half_sum + fold(ds[rows:quart_at], jnp.add)
            quart_sum = quart_sum + fold(ds[quart_at:], jnp.add)
            ds_low = ds.astype(BF)
            low[c * block : (c + 1) * block] = ds_low
            part = dot(jnp.concatenate([ds_low, probs.astype(BF)], axis=1), both, 1, 0)
            if c >= CHIPS:
                part_send[j, c - CHIPS] = part.astype(BF)
            else:
                own_sum[c] = part
            if c == 2 * CHIPS - 1:
                part_copy = copy(
                    part_send.at[j], part_got.at[j], part_ss.at[j], part_rs.at[j], sibling
                )
                part_copy.start()
        bias_total = jnp.where(
            bias_lane == my_head,
            jnp.where(bias_row == 0, jnp.sum(half_sum), jnp.sum(quart_sum)),
            bias_total,
        )
        kv = kv_all[j].reshape(2 * CHIPS * block, LANES)
        dq = (dot(kv, low[...], 0, 0)[:HD] * F32(HD**-0.5)).astype(BF)
        for dy in range(CHIPS):
            dq_send[j, dy] = dq[:, dy * rows : (dy + 1) * rows]
        dq_out[my_head] = dq[:, :rows]
        for dy in (1, 3, 2):
            c = copy(
                dq_send.at[j, dy],
                dq_out.at[my_head],
                dq_ss.at[j, dy],
                dq_rs.at[j, dy],
                device(x, z, chip(CHIPS - dy), core),
            )
            c.start()
            out_copies.append(c)
        part_copy.wait()
        for dy in (1, 3, 2, 0):
            done = (own_sum[dy] + part_got[j, dy].astype(F32)).astype(BF)
            if dy == 0:
                dkv_out[my_head] = done
                continue
            dkv_send[j, dy] = done
            c = copy(
                dkv_send.at[j, dy],
                dkv_out.at[my_head],
                dkv_ss.at[j, dy],
                dkv_rs.at[j, dy],
                device(x, z, chip(CHIPS - dy), core),
            )
            c.start()
            out_copies.append(c)

    bias_send[0] = bias_total
    copies = []
    for i in range(1, 2 * CHIPS):
        dy, p = divmod(i, 2)
        c = copy(
            bias_send.at[0],
            bias_clip.at[i],
            clip_ss.at[i],
            clip_rs.at[i],
            device(x, z, chip(dy), (core + p) % 2),
        )
        c.start()
        copies.append(c)
    for c in copies:
        c.wait()
    for i in range(1, 2 * CHIPS):
        bias_total = bias_total + bias_clip[i]

    def spread(total, count, me, at, slots, stage, ss, rs):
        if count == 1:
            return total
        bias_send[stage] = total
        slots[me] = total
        copies = []
        for d in range(1, count):
            c = copy(
                bias_send.at[stage], slots.at[me], ss.at[d], rs.at[d], at((me + d) % count)
            )
            c.start()
            copies.append(c)
        for c in copies:
            c.wait()
        total = slots[0]
        for d in range(1, count):
            total = total + slots[d]
        return total

    bias_total = spread(
        bias_total, n_x, x, lambda i: device(i, z, y, core), bias_x, 1, x_ss, x_rs
    )
    bias_total = spread(
        bias_total, n_z, z, lambda i: device(x, i, y, core), bias_z, 2, zz_ss, zz_rs
    )
    bias_out[...] = bias_total

    for c in kv_copies.values():
        c.wait_send()
    for c in sib_copies:
        c.wait_send()
    for c in fwd_copies.values():
        c.wait_send()
    for c in qa_copies.values():
        c.wait_send()
    for c in out_copies:
        c.wait()


def finish_kernel(
    half_rows,
    quart_rows,
    dq,
    dkv,
    bias,
    d_query,
    d_key,
    d_value,
    d_half_key,
    d_half_value,
    d_quart_key,
    d_quart_value,
    d_bias,
):
    heads = dq.shape[0]
    rows = d_key.shape[0]
    quart_at = dkv.shape[1] - 16
    for i in range(heads // 2):
        cols = slice(i * LANES, (i + 1) * LANES)
        d_query[:, cols] = dq[2 * i : 2 * i + 2].reshape(LANES, rows).T
        low, high = dkv[2 * i], dkv[2 * i + 1]
        for upper, outs in (
            (False, (d_key, d_half_key, d_quart_key)),
            (True, (d_value, d_half_value, d_quart_value)),
        ):
            both = joined(low, high, upper)
            outs[0][:, cols] = both[:rows]
            outs[1][:, cols] = both[rows : rows + half_rows]
            outs[2][:, cols] = both[quart_at : quart_at + quart_rows]
    d_bias[...] = bias[: d_bias.shape[0], : d_bias.shape[1]]


def shards(
    cur_query,
    cur_key,
    cur_value,
    grad_out,
    out_weight,
    half_key,
    half_value,
    quart_key,
    quart_value,
    cur_count,
    section_bias,
    n_x,
    n_z,
):
    rows, width = cur_query.shape
    half_rows, quart_rows = half_key.shape[0], quart_key.shape[0]
    heads = width // HD
    block = rows + 48
    anywhere = pl.BlockSpec(memory_space=pl.ANY)
    vmem = pl.BlockSpec(memory_space=pltpu.VMEM)
    smem = pl.BlockSpec(memory_space=pltpu.SMEM)
    dma = pltpu.SemaphoreType.DMA
    queries = CHIPS * rows
    shards_n = 2 * CHIPS
    pair = [dma((HEADS, CHIPS)), dma((HEADS, CHIPS))]
    triple = [dma((HEADS,)), dma((HEADS,))]
    dq, dkv, bias = pl.pallas_call(
        functools.partial(exchange_kernel, n_x, n_z),
        out_shape=(
            jax.ShapeDtypeStruct((heads, HD, rows), BF),
            jax.ShapeDtypeStruct((heads, block, LANES), BF),
            jax.ShapeDtypeStruct((8, LANES), F32),
        ),
        in_specs=[anywhere] * 5 + [vmem] * 4 + [smem] * 2,
        out_specs=(vmem, vmem, vmem),
        scratch_shapes=[
            pltpu.VMEM((rows, width), BF),
            pltpu.VMEM((rows, width), BF),
            pltpu.VMEM((rows, width), BF),
            pltpu.VMEM((rows, width), BF),
            pltpu.VMEM((rows, width), BF),
            pltpu.VMEM(out_weight.shape, BF),
            pltpu.VMEM((heads, block, LANES), BF),
            pltpu.VMEM((heads, rows, LANES), BF),
            pltpu.VMEM((HEADS, 2, CHIPS, block, LANES), BF),
            pltpu.VMEM((HEADS, CHIPS, rows, LANES), BF),
            pltpu.VMEM((shards_n, rows, LANES), F32),
            pltpu.VMEM((8, LANES), F32),
            pltpu.VMEM((shards_n, block, queries), F32),
            pltpu.VMEM((shards_n, block, queries), F32),
            pltpu.VMEM((shards_n * block, queries), BF),
            pltpu.VMEM((HEADS, CHIPS, block, LANES), BF),
            pltpu.VMEM((HEADS, CHIPS, block, LANES), BF),
            pltpu.VMEM((CHIPS, block, LANES), F32),
            pltpu.VMEM((HEADS, CHIPS, block, LANES), BF),
            pltpu.VMEM((HEADS, CHIPS, HD, rows), BF),
            pltpu.VMEM((3, 8, LANES), F32),
            pltpu.VMEM((shards_n, 8, LANES), F32),
            pltpu.VMEM((n_x, 8, LANES), F32),
            pltpu.VMEM((n_z, 8, LANES), F32),
            dma((5,)),
            dma((2,)),
            *pair,
            *triple,
            *pair,
            *pair,
            *triple,
            *pair,
            *pair,
            dma((shards_n,)),
            dma((shards_n,)),
            dma((n_x,)),
            dma((n_x,)),
            dma((n_z,)),
            dma((n_z,)),
        ],
        compiler_params=pltpu.CompilerParams(
            collective_id=0, has_side_effects=True, vmem_limit_bytes=48 << 20
        ),
        name="exchange",
    )(
        cur_query,
        cur_key,
        cur_value,
        grad_out,
        out_weight,
        half_key,
        half_value,
        quart_key,
        quart_value,
        cur_count,
        section_bias,
    )
    like = lambda a: jax.ShapeDtypeStruct(a.shape, a.dtype)
    return pl.pallas_call(
        functools.partial(finish_kernel, half_rows, quart_rows),
        out_shape=(
            like(cur_query),
            like(cur_key),
            like(cur_value),
            like(half_key),
            like(half_value),
            like(quart_key),
            like(quart_value),
            like(section_bias),
        ),
        in_specs=[vmem] * 3,
        out_specs=(vmem,) * 8,
        name="finish",
    )(dq, dkv, bias)


def solution(mesh):
    n_z = 4
    n_x = mesh.shape["seq"] // (2 * CHIPS * n_z)
    return jax.shard_map(
        functools.partial(shards, n_x=n_x, n_z=n_z),
        mesh=mesh,
        in_specs=(
            P("seq", "head"),
            P("seq", "head"),
            P("seq", "head"),
            P("seq", "head"),
            P(None, "head"),
            P("seq", "head"),
            P("seq", "head"),
            P("seq", "head"),
            P("seq", "head"),
            P(),
            P(None, "head"),
        ),
        out_specs=(
            P("seq", "head"),
            P("seq", "head"),
            P("seq", "head"),
            P("seq", "head"),
            P("seq", "head"),
            P("seq", "head"),
            P("seq", "head"),
            P(None, "head"),
        ),
        check_vma=False,
    )
```

time: 662 us -> 62.5 us (0.09)
  blocking collectives: 357 us -> 0 us
  waiting for transfers between devices: 99.3 us -> 0 us
  local copies, waits for them, and re-layouts: 101 us -> 11.9 us
  Pallas kernels: 0 us -> 49.5 us
  other arithmetic: 44.9 us -> 0 us
  matrix products: 40.3 us -> 0 us
  starting transfers between devices: 11.4 us -> 0 us
    psum x1 -> x0, blocking collectives: 351 us -> none  [shards(): d_section_bias = lax.psum(bias_term, 'seq')]
    ppermute x6 -> x0, waiting for transfers between devices: 99.3 us -> none  [partner_2(): return lax.ppermute(value, axis, pairs)]
    pallas_call x0 -> x2, Pallas kernels: none -> 49.5 us  [the longest x1 47.4 us: shards(): pl.pallas_call(functools.partial(exchange_kernel, n_x, n_z), out_shape=(j...]
    another operation x7 -> x0, local copies, waits for them, and re-layouts: 45.4 us -> none  [the longest x2 45.2 us: shards(): jnp.stack([jnp.concatenate(key_parts, axis=1), jnp.concatenate(value_part...]
    dot_general x38 -> x0, matrix products: 27.4 us -> none  [the longest x6 13.4 us: shards(): jnp.einsum('qhd,khd->hqk', adjoint_pair, value_pair, preferred_element_ty...]
    convert_element_type x11 -> x0, other arithmetic: 24.4 us -> none  [the longest x1 9.83 us: shards(): summed = jnp.stack([jnp.concatenate(key_parts, axis=1), jnp.concatenate(v...]
    slice x32 -> x0, local copies, waits for them, and re-layouts: 21.1 us -> none  [the longest x7 8.61 us: shards(): all_values[:, first_col:first_col + pair_width].reshape(-1, pair_size, HD)]
    reshape x18 -> x0, local copies, waits for them, and re-layouts: 16.7 us -> none  [the longest x6 8.53 us: shards(): value_parts.append(value_grad.astype(jnp.bfloat16).reshape(-1, pair_width))]
  transfers between devices with their start and end apart: 6 -> 0, of which waited for: 5 -> 0; matrix products, arithmetic and copies ran while one was open for 2% -> 0% of each run, Pallas kernels for 0% -> 0%
where the time goes in v1:
time: 62.5 us; the launch traced here: 62 us
  Pallas kernels  49.5 us (79%)
  local copies, waits for them, and re-layouts  11.9 us (19%)
  between operations  0.66 us (1%)
    pallas_call x1, Pallas kernels, shards(): pl.pallas_call(functools.partial(exchange_kernel, n_x, n_z), out_shape=(j...  47.4 us
    unnamed x27, local copies, waits for them, and re-layouts  11.9 us
    pallas_call x1, Pallas kernels, shards(): pl.pallas_call(functools.partial(finish_kernel, half_rows, quart_rows), o...  2.11 us

profile of v1, /device:TPU:1, one launch (start us, length us, event | category | flops | bytes accessed | tf_op | source)
XLA Modules:
  0.0 62.0 jit_solution(17163783341019993919)
XLA Ops:
  0.6 0.8 %copy.19.counts = s32[16,8]{1,0:T(8,128)S(1)} copy(s32[16,8]{0,1:T(8,128)} %param.20) | data formatting | bytes 1024 | tf_op args[9]
  1.4 0.0 copy-start
  1.4 1.7 %copy-done = bf16[1536,768]{1,0:T(8,128)(2,1)S(1)} copy-done((bf16[1536,768]{1,0:T(8,128)(2,1)S(1)}, bf16[1536,768]{1,0:T(8,128)(2,1)}, u32[]{:S(2)}) %copy-start) | copy-done | bytes 2359320
  3.1 0.0 copy-start.2
  3.1 0.9 %copy-done.2 = bf16[128,768]{1,0:T(8,128)(2,1)S(1)} copy-done((bf16[128,768]{1,0:T(8,128)(2,1)S(1)}, bf16[128,768]{1,0:T(8,128)(2,1)}, u32[]{:S(2)}) %copy-start.2) | copy-done | bytes 196632
  4.0 0.0 copy-start.3
  4.0 0.9 %copy-done.3 = bf16[128,768]{1,0:T(8,128)(2,1)S(1)} copy-done((bf16[128,768]{1,0:T(8,128)(2,1)S(1)}, bf16[128,768]{1,0:T(8,128)(2,1)}, u32[]{:S(2)}) %copy-start.3) | copy-done | bytes 196632
  4.9 0.0 copy-start.4
  4.9 0.9 %copy-done.4 = bf16[128,768]{1,0:T(8,128)(2,1)S(1)} copy-done((bf16[128,768]{1,0:T(8,128)(2,1)S(1)}, bf16[128,768]{1,0:T(8,128)(2,1)}, u32[]{:S(2)}) %copy-start.4) | copy-done | bytes 196632
  5.8 0.0 copy-start.5
  5.8 0.9 %copy-done.5 = bf16[128,768]{1,0:T(8,128)(2,1)S(1)} copy-done((bf16[128,768]{1,0:T(8,128)(2,1)S(1)}, bf16[128,768]{1,0:T(8,128)(2,1)}, u32[]{:S(2)}) %copy-start.5) | copy-done | bytes 196632
  6.8 0.0 copy-start.7
  6.8 0.8 %copy-done.7 = bf16[30,768]{1,0:T(8,128)(2,1)S(1)} copy-done((bf16[30,768]{1,0:T(8,128)(2,1)S(1)}, bf16[30,768]{1,0:T(8,128)(2,1)}, u32[]{:S(2)}) %copy-start.7) | copy-done | bytes 46104
  7.6 0.8 %copy-done.8 = bf16[30,768]{1,0:T(8,128)(2,1)S(1)} copy-done((bf16[30,768]{1,0:T(8,128)(2,1)S(1)}, bf16[30,768]{1,0:T(8,128)(2,1)}, u32[]{:S(2)}) %copy-start.8) | copy-done | bytes 46104
  8.4 0.0 copy-start.9
  8.4 0.7 %copy-done.9 = bf16[8,768]{1,0:T(8,128)(2,1)S(1)} copy-done((bf16[8,768]{1,0:T(8,128)(2,1)S(1)}, bf16[8,768]{1,0:T(8,128)(2,1)}, u32[]{:S(2)}) %copy-start.9) | copy-done | bytes 12312
  9.1 0.7 %copy-done.10 = bf16[8,768]{1,0:T(8,128)(2,1)S(1)} copy-done((bf16[8,768]{1,0:T(8,128)(2,1)S(1)}, bf16[8,768]{1,0:T(8,128)(2,1)}, u32[]{:S(2)}) %copy-start.10) | copy-done | bytes 12312
  9.8 0.7 %copy-done.12 = f32[2,12]{1,0:T(2,128)S(1)} copy-done((f32[2,12]{1,0:T(2,128)S(1)}, f32[2,12]{1,0:T(2,128)}, u32[]{:S(2)}) %copy-start.12) | copy-done | bytes 120
  10.5 47.4 %exchange.1 = (bf16[12,64,128]{2,1,0:T(8,128)(2,1)S(1)}, bf16[12,176,128]{2,1,0:T(8,128)(2,1)S(1)}, f32[8,128]{1,0:T(8,128)S(1)}) custom-call(bf16[128,768]{1,0:T(8,128)(2,1)S(1)} %copy-done.2, bf16[128,768]{1,0:T(8,128)(2,1)S(1)} %copy-done.3, bf16[128,768]{1,0:T(8,128)(2,1)S(1)} %copy-done.4, bf16[128,768]{1,0:T(8,128)(2,1)S(1)} %copy-done.5, ...), custom_call_target="tpu_custom_call" | custom-call | tf_op jit(solution)/shard_map/exchange/pallas_call | solution.py:473
  57.8 0.0 copy-start.1
  57.9 0.8 %copy-done.1 = bf16[12,176,128]{2,1,0:T(8,128)(2,1)} copy-done((bf16[12,176,128]{2,1,0:T(8,128)(2,1)}, bf16[12,176,128]{2,1,0:T(8,128)(2,1)S(1)}, u32[]{:S(2)}) %copy-start.1) | copy-done | bytes 540696
  58.6 0.7 %copy-done.6 = bf16[12,64,128]{2,1,0:T(8,128)(2,1)} copy-done((bf16[12,64,128]{2,1,0:T(8,128)(2,1)}, bf16[12,64,128]{2,1,0:T(8,128)(2,1)S(1)}, u32[]{:S(2)}) %copy-start.6) | copy-done | bytes 196632
  59.3 0.6 copy-done.11
  59.9 2.1 %finish.1 = (bf16[128,768]{1,0:T(8,128)(2,1)}, bf16[128,768]{1,0:T(8,128)(2,1)}, bf16[128,768]{1,0:T(8,128)(2,1)}, bf16[30,768]{1,0:T(8,128)(2,1)}, bf16[30,768]...) custom-call(bf16[12,64,128]{2,1,0:T(8,128)(2,1)} %copy-done.6, ...), custom_call_target="tpu_custom_call" | custom-call | tf_op jit(solution)/shard_map/finish/pallas_call | solution.py:541
  (5 shorter events, 0.0 us)
Async XLA Ops:
  1.4 1.7 %copy-start = (bf16[1536,768]{1,0:T(8,128)(2,1)S(1)}, bf16[1536,768]{1,0:T(8,128)(2,1)}, u32[]{:S(2)}) copy-start(bf16[1536,768]{1,0:T(8,128)(2,1)} %weight_hbm.1) | copy-start | bytes 7077892
  3.1 0.9 %copy-start.2 = (bf16[128,768]{1,0:T(8,128)(2,1)S(1)}, bf16[128,768]{1,0:T(8,128)(2,1)}, u32[]{:S(2)}) copy-start(bf16[128,768]{1,0:T(8,128)(2,1)} %query_hbm.1) | copy-start | bytes 589828
  4.0 0.9 %copy-start.3 = (bf16[128,768]{1,0:T(8,128)(2,1)S(1)}, bf16[128,768]{1,0:T(8,128)(2,1)}, u32[]{:S(2)}) copy-start(bf16[128,768]{1,0:T(8,128)(2,1)} %key_hbm.1) | copy-start | bytes 589828
  4.9 0.9 %copy-start.4 = (bf16[128,768]{1,0:T(8,128)(2,1)S(1)}, bf16[128,768]{1,0:T(8,128)(2,1)}, u32[]{:S(2)}) copy-start(bf16[128,768]{1,0:T(8,128)(2,1)} %value_hbm.1) | copy-start | bytes 589828
  5.8 0.9 %copy-start.5 = (bf16[128,768]{1,0:T(8,128)(2,1)S(1)}, bf16[128,768]{1,0:T(8,128)(2,1)}, u32[]{:S(2)}) copy-start(bf16[128,768]{1,0:T(8,128)(2,1)} %grad_hbm.1) | copy-start | bytes 589828
  6.8 0.8 %copy-start.7 = (bf16[30,768]{1,0:T(8,128)(2,1)S(1)}, bf16[30,768]{1,0:T(8,128)(2,1)}, u32[]{:S(2)}) copy-start(bf16[30,768]{1,0:T(8,128)(2,1)} %half_key.1) | copy-start | bytes 138244
  7.6 0.8 %copy-start.8 = (bf16[30,768]{1,0:T(8,128)(2,1)S(1)}, bf16[30,768]{1,0:T(8,128)(2,1)}, u32[]{:S(2)}) copy-start(bf16[30,768]{1,0:T(8,128)(2,1)} %half_value.1) | copy-start | bytes 138244
  8.4 0.7 %copy-start.9 = (bf16[8,768]{1,0:T(8,128)(2,1)S(1)}, bf16[8,768]{1,0:T(8,128)(2,1)}, u32[]{:S(2)}) copy-start(bf16[8,768]{1,0:T(8,128)(2,1)} %quart_key.1) | copy-start | bytes 36868
  9.1 0.7 %copy-start.10 = (bf16[8,768]{1,0:T(8,128)(2,1)S(1)}, bf16[8,768]{1,0:T(8,128)(2,1)}, u32[]{:S(2)}) copy-start(bf16[8,768]{1,0:T(8,128)(2,1)} %quart_value.1) | copy-start | bytes 36868
  9.8 0.7 %copy-start.12 = (f32[2,12]{1,0:T(2,128)S(1)}, f32[2,12]{1,0:T(2,128)}, u32[]{:S(2)}) copy-start(f32[2,12]{1,0:T(2,128)} %section_bias.1) | copy-start | bytes 292
  57.8 0.8 %copy-start.1 = (bf16[12,176,128]{2,1,0:T(8,128)(2,1)}, bf16[12,176,128]{2,1,0:T(8,128)(2,1)S(1)}, u32[]{:S(2)}) copy-start(bf16[12,176,128]{2,1,0:T(8,128)(2,1)S(1)} %get-tuple-element.12.dkv) | copy-start | bytes 1622020
  58.6 0.7 %copy-start.6 = (bf16[12,64,128]{2,1,0:T(8,128)(2,1)}, bf16[12,64,128]{2,1,0:T(8,128)(2,1)S(1)}, u32[]{:S(2)}) copy-start(bf16[12,64,128]{2,1,0:T(8,128)(2,1)S(1)} %get-tuple-element.11.dq) | copy-start | bytes 589828
  59.3 0.6 copy-start.11

commit v2 on v1

v2 whole, which is shorter than its diff:
```python
import functools

import jax
import jax.numpy as jnp
from jax import lax
from jax.experimental import pallas as pl
from jax.experimental.pallas import tpu as pltpu
from jax.sharding import PartitionSpec as P

HD = 64
LANES = 128
CHIPS = 4
HEADS = 3
FAR = 3
MESH = pl.DeviceIdType.MESH
BF = jnp.bfloat16
F32 = jnp.float32


def dot(a, b, ca, cb):
    return lax.dot_general(a, b, (((ca,), (cb,)), ((), ())), preferred_element_type=F32)


def joined(a, head_a, b, head_b):
    return jnp.concatenate(
        [a[:, head_a * HD : (head_a + 1) * HD], b[:, head_b * HD : (head_b + 1) * HD]], axis=1
    )


def exchange_kernel(
    n_x,
    n_z,
    query_hbm,
    key_hbm,
    value_hbm,
    grad_hbm,
    weight_hbm,
    half_key_hbm,
    half_value_hbm,
    quart_key_hbm,
    quart_value_hbm,
    counts_hbm,
    section_bias_hbm,
    dq_out,
    dkv_out,
    bias_out,
    query,
    key,
    value,
    grad,
    grad_far,
    weight,
    half_key,
    half_value,
    quart_key,
    quart_value,
    counts,
    section_bias,
    kv_send,
    qa_send,
    kv_all,
    qa_all,
    count_bias,
    tops,
    scores,
    d_probs,
    low,
    part_send,
    part_got,
    own_sum,
    dkv_send,
    dq_send,
    bias_send,
    bias_zc,
    bias_xy,
    load_sem,
    z_ss,
    z_rs,
    kv_ss,
    kv_rs,
    sib_ss,
    sib_rs,
    fwd_ss,
    fwd_rs,
    qa_ss,
    qa_rs,
    part_ss,
    part_rs,
    dkv_ss,
    dkv_rs,
    dq_ss,
    dq_rs,
    zc_ss,
    zc_rs,
    xy_ss,
    xy_rs,
):
    rows = query_hbm.shape[0]
    half_rows = half_key_hbm.shape[0]
    quart_rows = quart_key_hbm.shape[0]
    width = query_hbm.shape[1]
    block = kv_send.shape[1]
    quart_at = block - 16
    heads = width // HD
    seq = lax.axis_index("seq")
    head = lax.axis_index("head")
    core = seq % 2
    y = seq // 2 % CHIPS
    z = seq // 8 % n_z
    x = seq // (8 * n_z)
    clip = seq // 8

    def device(x, z, y, core):
        return ((x * n_z + z) * CHIPS + y) * 2 + core

    def chip(dy):
        return (y + dy) % CHIPS

    def copy(src, dst, ss, rs, seq_to, head_to=None):
        return pltpu.make_async_remote_copy(
            src_ref=src,
            dst_ref=dst,
            send_sem=ss,
            recv_sem=rs,
            device_id={"seq": seq_to, "head": head if head_to is None else head_to},
            device_id_type=MESH,
        )

    loads = [
        pltpu.make_async_copy(a, b, load_sem.at[i])
        for i, (a, b) in enumerate(
            [
                (query_hbm, query),
                (key_hbm, key),
                (value_hbm, value),
                (half_key_hbm, half_key),
                (half_value_hbm, half_value),
                (quart_key_hbm, quart_key),
                (quart_value_hbm, quart_value),
                (counts_hbm, counts),
                (section_bias_hbm, section_bias),
                (grad_hbm, grad),
                (weight_hbm, weight),
            ]
        )
    ]
    for load in loads:
        load.start()

    sibling = device(x, z, y, 1 - core)
    zc_peers = [
        device(x, (z + d) % n_z, y, (core + p) % 2) for d in range(n_z) for p in range(2)
    ][1:]
    xy_peers = [device((x + d) % n_x, z, chip(dy), core) for d in range(n_x) for dy in range(CHIPS)][1:]
    partners = [(seq, 1 - head)] + [(peer, head) for peer in zc_peers + xy_peers]
    barrier = pltpu.get_barrier_semaphore()
    for seq_to, head_to in partners:
        pl.semaphore_signal(
            barrier, inc=1, device_id={"seq": seq_to, "head": head_to}, device_id_type=MESH
        )

    for load in loads[:7]:
        load.wait()
    zeros = jnp.zeros((block - rows, LANES), BF)
    for h in range(heads):
        first, second = (value, key) if h % HEADS == 1 else (key, value)
        kv_send[h, :rows] = joined(first, h, second, h)
        kv_send[h, rows:] = zeros
        first, second = (half_value, half_key) if h % HEADS == 1 else (half_key, half_value)
        kv_send[h, rows : rows + half_rows] = joined(first, h, second, h)
        first, second = (quart_value, quart_key) if h % HEADS == 1 else (quart_key, quart_value)
        kv_send[h, quart_at : quart_at + quart_rows] = joined(first, h, second, h)
    query[...] = query[...] * BF(HD**-0.5)
    for c in range(CHIPS):
        qa_send[HEADS * c] = joined(query, HEADS * c, query, HEADS * c + 1)

    pl.semaphore_wait(barrier, len(partners))

    far_cols = width // FAR
    z_copies = []
    for i in range(FAR):
        cols = slice(i * far_cols, (i + 1) * far_cols)
        c = copy(
            grad_hbm.at[:, cols], grad_far.at[:, cols], z_ss.at[i], z_rs.at[i], seq, 1 - head
        )
        c.start()
        z_copies.append(c)
    qa_copies = {}

    def send_tile(t):
        for dy in (1, 3, 2):
            c = copy(
                qa_send.at[HEADS * chip(dy) + t],
                qa_all.at[t, dy],
                qa_ss.at[t, dy],
                qa_rs.at[t, dy],
                device(x, z, chip(dy), core),
            )
            c.start()
            qa_copies[t, dy] = c
        qa_all[t, 0] = qa_send[HEADS * y + t]

    send_tile(0)
    kv_copies = {}
    sib_copies = []
    for j in range(HEADS):
        for dy in (1, 3, 2):
            c = copy(
                kv_send.at[HEADS * chip(dy) + j],
                kv_all.at[j, 0, dy],
                kv_ss.at[j, dy],
                kv_rs.at[j, dy],
                device(x, z, chip(dy), core),
            )
            c.start()
            kv_copies[j, dy] = c
        c = copy(
            kv_send.at[HEADS * y + j], kv_all.at[j, 1, 0], sib_ss.at[j], sib_rs.at[j], sibling
        )
        c.start()
        sib_copies.append(c)
        kv_all[j, 0, 0] = kv_send[HEADS * y + j]

    loads[7].wait()
    loads[8].wait()
    row_id = lax.broadcasted_iota(jnp.int32, (rows, LANES), 0)
    for c in range(2 * CHIPS):
        p, dy = divmod(c, CHIPS)
        shard = 2 * chip(CHIPS - dy) + (core if p == 0 else 1 - core)
        count_bias[c] = jnp.where(row_id < counts[shard, clip], F32(0), F32(-1e30))

    loads[9].wait()
    loads[10].wait()
    adjoint = dot(grad[...], weight[pl.ds(pl.multiple_of(head * width, LANES), width), :], 1, 0)

    fwd_copies = {}

    def forward(j):
        for dy in (1, 3, 2):
            kv_copies[j, dy].wait_recv()
            c = copy(
                kv_all.at[j, 0, dy],
                kv_all.at[j, 1, dy],
                fwd_ss.at[j, dy],
                fwd_rs.at[j, dy],
                sibling,
            )
            c.start()
            fwd_copies[j, dy] = c

    forward(0)
    forward(1)
    for i in range(FAR):
        z_copies[i].wait_recv()
        at = pl.multiple_of((1 - head) * width + i * far_cols, LANES)
        adjoint += dot(
            grad_far[:, i * far_cols : (i + 1) * far_cols], weight[pl.ds(at, far_cols), :], 1, 0
        )
    own_count = counts[2 * y + core, clip]
    row_wide = lax.broadcasted_iota(jnp.int32, (rows, width), 0)
    adjoint = jnp.where(row_wide < own_count, adjoint, F32(0)).astype(BF)
    for c in range(CHIPS):
        qa_send[HEADS * c + 1] = joined(adjoint, HEADS * c + 1, adjoint, HEADS * c)
    send_tile(1)
    for c in range(CHIPS):
        qa_send[HEADS * c + 2] = joined(query, HEADS * c + 2, adjoint, HEADS * c + 2)
    send_tile(2)
    forward(2)

    bias_row = lax.broadcasted_iota(jnp.int32, (8, LANES), 0)
    bias_lane = lax.broadcasted_iota(jnp.int32, (8, LANES), 1)
    hist_id = lax.broadcasted_iota(jnp.int32, (block - rows, LANES), 0)
    queries = CHIPS * rows
    groups = queries // LANES
    low_lane = lax.broadcasted_iota(jnp.int32, (queries, LANES), 1) < HD

    def fold(t, op):
        total = t[:8]
        for r in range(8, t.shape[0], 8):
            total = op(total, t[r : r + 8])
        return total

    def wait_tile(t):
        for dy in (1, 3, 2):
            qa_copies[t, dy].wait_recv()

    def wait_keys(j):
        for dy in (1, 3, 2):
            fwd_copies[j, dy].wait_recv()
        sib_copies[j].wait_recv()

    def query_part(j):
        tile = qa_all[2 if j == 2 else 0].reshape(queries, LANES)
        return jnp.where(low_lane, BF(0), tile) if j == 1 else jnp.where(low_lane, tile, BF(0))

    def adjoint_part(j):
        tile = qa_all[2 if j == 2 else 1].reshape(queries, LANES)
        return jnp.where(low_lane, tile, BF(0)) if j == 1 else jnp.where(low_lane, BF(0), tile)

    def score_pass(j):
        my_head = HEADS * y + j
        half_bias = section_bias[0, my_head]
        quart_bias = section_bias[1, my_head]
        hist_bias = jnp.where(
            hist_id < half_rows,
            half_bias,
            jnp.where(
                (hist_id >= quart_at - rows) & (hist_id < quart_at - rows + quart_rows),
                quart_bias,
                F32(-1e30),
            ),
        )
        q_part = query_part(j)
        top = jnp.full((8, queries), -3e38, F32)
        for c in range(2 * CHIPS):
            s = dot(kv_all[j, c // CHIPS, c % CHIPS], q_part, 1, 1)
            bias = jnp.concatenate([count_bias[c], hist_bias], axis=0)
            s = s + jnp.concatenate([bias] * groups, axis=1)
            scores[j, c] = s
            top = jnp.maximum(top, fold(s, jnp.maximum))
        tops[j] = top

    def dscore_pass(j):
        a_part = adjoint_part(j)
        top = jnp.max(tops[j], axis=0, keepdims=True)
        total = jnp.zeros((8, queries), F32)
        delta = jnp.zeros((8, queries), F32)
        for c in range(2 * CHIPS):
            dp = dot(kv_all[j, c // CHIPS, c % CHIPS], a_part, 1, 1)
            e = jnp.exp(scores[j, c] - top)
            scores[j, c] = e
            d_probs[c] = dp
            total = total + fold(e, jnp.add)
            delta = delta + fold(e * dp, jnp.add)
        inverse = 1.0 / jnp.sum(total, axis=0, keepdims=True)
        delta = jnp.sum(delta, axis=0, keepdims=True) * inverse
        half_sum = jnp.zeros((8, queries), F32)
        quart_sum = jnp.zeros((8, queries), F32)
        for c in range(2 * CHIPS):
            probs = scores[j, c] * inverse
            ds = probs * (d_probs[c] - delta)
            half_sum = half_sum + fold(ds[rows:quart_at], jnp.add)
            quart_sum = quart_sum + fold(ds[quart_at:], jnp.add)
            low[j, c * block : (c + 1) * block, :queries] = ds.astype(BF)
            low[j, c * block : (c + 1) * block, queries:] = probs.astype(BF)
        return jnp.where(
            bias_lane == HEADS * y + j,
            jnp.where(bias_row == 0, jnp.sum(half_sum), jnp.sum(quart_sum)),
            F32(0),
        )

    part_copies = {}
    out_copies = []
    own_copies = []

    def products(j):
        my_head = HEADS * y + j
        near = CHIPS * block
        both = jnp.concatenate([query_part(j), adjoint_part(j)], axis=0)
        kv = kv_all[j].reshape(2 * near, LANES)
        at = HD if j == 1 else 0
        dq = (dot(kv, low[j, :, :queries], 0, 0)[at : at + HD] * F32(HD**-0.5)).astype(BF)
        for dy in range(CHIPS):
            dq_send[j, dy] = dq[:, dy * rows : (dy + 1) * rows]
        for dy in (1, 3, 2):
            c = copy(
                dq_send.at[j, dy],
                dq_out.at[my_head],
                dq_ss.at[j, dy],
                dq_rs.at[j, dy],
                device(x, z, chip(CHIPS - dy), core),
            )
            c.start()
            out_copies.append(c)
        c = pltpu.make_async_copy(dq_send.at[j, 0], dq_out.at[my_head], dq_ss.at[j, 0])
        c.start()
        own_copies.append(c)
        part_send[j] = dot(low[j, near:], both, 1, 0).astype(BF)
        c = copy(part_send.at[j], part_got.at[j], part_ss.at[j], part_rs.at[j], sibling)
        c.start()
        part_copies[j] = c
        own_sum[j] = dot(low[j, :near], both, 1, 0)

    def send_keys(j):
        my_head = HEADS * y + j
        part_copies[j].wait()
        for dy in (1, 3, 2, 0):
            at = slice(dy * block, (dy + 1) * block)
            dkv_send[j, dy] = (own_sum[j, at] + part_got[j, at].astype(F32)).astype(BF)
            if dy == 0:
                c = pltpu.make_async_copy(dkv_send.at[j, 0], dkv_out.at[my_head], dkv_ss.at[j, 0])
                c.start()
                own_copies.append(c)
                continue
            c = copy(
                dkv_send.at[j, dy],
                dkv_out.at[my_head],
                dkv_ss.at[j, dy],
                dkv_rs.at[j, dy],
                device(x, z, chip(CHIPS - dy), core),
            )
            c.start()
            out_copies.append(c)

    def spread(total, stage, peers, slots, me, ss, rs):
        bias_send[stage] = total
        slots[me] = total
        copies = []
        for i, peer in enumerate(peers):
            c = copy(bias_send.at[stage], slots.at[me], ss.at[i], rs.at[i], peer)
            c.start()
            copies.append(c)
        return copies

    def gathered(slots, copies):
        for c in copies:
            c.wait()
        total = slots[0]
        for i in range(1, len(copies) + 1):
            total = total + slots[i]
        return total

    wait_tile(0)
    wait_keys(0)
    score_pass(0)
    wait_keys(1)
    score_pass(1)
    wait_tile(1)
    bias_total = dscore_pass(0)
    products(0)
    bias_total = bias_total + dscore_pass(1)
    send_keys(0)
    wait_keys(2)
    wait_tile(2)
    score_pass(2)
    bias_total = bias_total + dscore_pass(2)
    zc_copies = spread(bias_total, 0, zc_peers, bias_zc, 2 * z + core, zc_ss, zc_rs)
    products(1)
    products(2)
    send_keys(1)
    send_keys(2)
    bias_total = gathered(bias_zc, zc_copies)
    xy_copies = spread(bias_total, 1, xy_peers, bias_xy, CHIPS * x + y, xy_ss, xy_rs)
    bias_out[...] = gathered(bias_xy, xy_copies)

    for c in kv_copies.values():
        c.wait_send()
    for c in sib_copies:
        c.wait_send()
    for c in fwd_copies.values():
        c.wait_send()
    for c in qa_copies.values():
        c.wait_send()
    for c in z_copies:
        c.wait_send()
    for c in own_copies + out_copies:
        c.wait()


def finish_kernel(
    half_rows,
    quart_rows,
    dq,
    dkv,
    bias,
    d_query,
    d_key,
    d_value,
    d_half_key,
    d_half_value,
    d_quart_key,
    d_quart_value,
    d_bias,
):
    heads = dq.shape[0]
    rows = d_key.shape[0]
    quart_at = dkv.shape[1] - 16
    for i in range(heads // 2):
        cols = slice(i * LANES, (i + 1) * LANES)
        d_query[:, cols] = dq[2 * i : 2 * i + 2].reshape(LANES, rows).T
        low, high = dkv[2 * i], dkv[2 * i + 1]
        swap_low, swap_high = 2 * i % HEADS == 1, (2 * i + 1) % HEADS == 1
        for value, outs in (
            (0, (d_key, d_half_key, d_quart_key)),
            (1, (d_value, d_half_value, d_quart_value)),
        ):
            both = joined(low, value ^ swap_low, high, value ^ swap_high)
            outs[0][:, cols] = both[:rows]
            outs[1][:, cols] = both[rows : rows + half_rows]
            outs[2][:, cols] = both[quart_at : quart_at + quart_rows]
    d_bias[...] = bias[: d_bias.shape[0], : d_bias.shape[1]]


def shards(
    cur_query,
    cur_key,
    cur_value,
    grad_out,
    out_weight,
    half_key,
    half_value,
    quart_key,
    quart_value,
    cur_count,
    section_bias,
    n_x,
    n_z,
):
    rows, width = cur_query.shape
    half_rows, quart_rows = half_key.shape[0], quart_key.shape[0]
    heads = width // HD
    block = rows + 48
    counts = cur_count.T
    hbm = pl.BlockSpec(memory_space=pltpu.HBM)
    vmem = pl.BlockSpec(memory_space=pltpu.VMEM)
    dma = pltpu.SemaphoreType.DMA
    queries = CHIPS * rows
    shards_n = 2 * CHIPS
    pair = [dma((HEADS, CHIPS)), dma((HEADS, CHIPS))]
    triple = [dma((HEADS,)), dma((HEADS,))]
    dq, dkv, bias = pl.pallas_call(
        functools.partial(exchange_kernel, n_x, n_z),
        out_shape=(
            jax.ShapeDtypeStruct((heads, HD, rows), BF),
            jax.ShapeDtypeStruct((heads, block, LANES), BF),
            jax.ShapeDtypeStruct((8, LANES), F32),
        ),
        in_specs=[hbm] * 11,
        out_specs=(hbm, hbm, vmem),
        scratch_shapes=[
            pltpu.VMEM((rows, width), BF),
            pltpu.VMEM((rows, width), BF),
            pltpu.VMEM((rows, width), BF),
            pltpu.VMEM((rows, width), BF),
            pltpu.VMEM((rows, width), BF),
            pltpu.VMEM(out_weight.shape, BF),
            pltpu.VMEM(half_key.shape, BF),
            pltpu.VMEM(half_value.shape, BF),
            pltpu.VMEM(quart_key.shape, BF),
            pltpu.VMEM(quart_value.shape, BF),
            pltpu.SMEM(counts.shape, jnp.int32),
            pltpu.SMEM(section_bias.shape, F32),
            pltpu.VMEM((heads, block, LANES), BF),
            pltpu.VMEM((heads, rows, LANES), BF),
            pltpu.VMEM((HEADS, 2, CHIPS, block, LANES), BF),
            pltpu.VMEM((HEADS, CHIPS, rows, LANES), BF),
            pltpu.VMEM((shards_n, rows, LANES), F32),
            pltpu.VMEM((HEADS, 8, queries), F32),
            pltpu.VMEM((HEADS, shards_n, block, queries), F32),
            pltpu.VMEM((shards_n, block, queries), F32),
            pltpu.VMEM((HEADS, shards_n * block, 2 * queries), BF),
            pltpu.VMEM((HEADS, CHIPS * block, LANES), BF),
            pltpu.VMEM((HEADS, CHIPS * block, LANES), BF),
            pltpu.VMEM((HEADS, CHIPS * block, LANES), F32),
            pltpu.VMEM((HEADS, CHIPS, block, LANES), BF),
            pltpu.VMEM((HEADS, CHIPS, HD, rows), BF),
            pltpu.VMEM((2, 8, LANES), F32),
            pltpu.VMEM((2 * n_z, 8, LANES), F32),
            pltpu.VMEM((n_x * CHIPS, 8, LANES), F32),
            dma((11,)),
            dma((FAR,)),
            dma((FAR,)),
            *pair,
            *triple,
            *pair,
            *pair,
            *triple,
            *pair,
            *pair,
            dma((2 * n_z,)),
            dma((2 * n_z,)),
            dma((n_x * CHIPS,)),
            dma((n_x * CHIPS,)),
        ],
        compiler_params=pltpu.CompilerParams(
            collective_id=0, has_side_effects=True, vmem_limit_bytes=62 << 20
        ),
        name="exchange",
    )(
        cur_query,
        cur_key,
        cur_value,
        grad_out,
        out_weight,
        half_key,
        half_value,
        quart_key,
        quart_value,
        counts,
        section_bias,
    )
    like = lambda a: jax.ShapeDtypeStruct(a.shape, a.dtype)
    return pl.pallas_call(
        functools.partial(finish_kernel, half_rows, quart_rows),
        out_shape=(
            like(cur_query),
            like(cur_key),
            like(cur_value),
            like(half_key),
            like(half_value),
            like(quart_key),
            like(quart_value),
            like(section_bias),
        ),
        in_specs=[vmem] * 3,
        out_specs=(vmem,) * 8,
        compiler_params=pltpu.CompilerParams(vmem_limit_bytes=62 << 20),
        name="finish",
    )(dq, dkv, bias)


def solution(mesh):
    n_z = 4
    n_x = mesh.shape["seq"] // (2 * CHIPS * n_z)
    return jax.shard_map(
        functools.partial(shards, n_x=n_x, n_z=n_z),
        mesh=mesh,
        in_specs=(
            P("seq", "head"),
            P("seq", "head"),
            P("seq", "head"),
            P("seq", "head"),
            P(None, "head"),
            P("seq", "head"),
            P("seq", "head"),
            P("seq", "head"),
            P("seq", "head"),
            P(),
            P(None, "head"),
        ),
        out_specs=(
            P("seq", "head"),
            P("seq", "head"),
            P("seq", "head"),
            P("seq", "head"),
            P("seq", "head"),
            P("seq", "head"),
            P("seq", "head"),
            P(None, "head"),
        ),
        check_vma=False,
    )
```

time: 62.5 us -> 44.2 us (0.71)
  local copies, waits for them, and re-layouts: 11.9 us -> 0 us
  Pallas kernels: 49.5 us -> 43.5 us
    unnamed x27 -> x0, local copies, waits for them, and re-layouts: 11.9 us -> none
    pallas_call x1, Pallas kernels: 47.4 us -> 41.3 us  [shards(): pl.pallas_call(functools.partial(exchange_kernel, n_x, n_z), out_shape=(j...]
where the time goes in v2:
time: 44.2 us; the launch traced here: 44.1 us
  Pallas kernels  43.5 us (98%)
  between operations  0.65 us (1%)
    pallas_call x1, Pallas kernels, shards(): pl.pallas_call(functools.partial(exchange_kernel, n_x, n_z), out_shape=(j...  41.3 us
    pallas_call x1, Pallas kernels, shards(): pl.pallas_call(functools.partial(finish_kernel, half_rows, quart_rows), o...  2.13 us

profile of v2, /device:TPU:1, one launch (start us, length us, event | category | flops | bytes accessed | tf_op | source)
XLA Modules:
  0.0 44.1 jit_solution(10828990102307574183)
XLA Ops:
  0.6 41.3 %exchange.1 = (bf16[12,64,128]{2,1,0:T(8,128)(2,1)}, bf16[12,176,128]{2,1,0:T(8,128)(2,1)}, f32[8,128]{1,0:T(8,128)}) custom-call(bf16[128,768]{1,0:T(8,128)(2,1)} %query_hbm.1, bf16[128,768]{1,0:T(8,128)(2,1)} %key_hbm.1, bf16[128,768]{1,0:T(8,128)(2,1)} %value_hbm.1, bf16[128,768]{1,0:T(8,128)(2,1)} %grad_hbm.1, bf16[1536,768]{1,0:T(8,128)(2,1)} %weight_hbm.1, ...), custom_call_target="tpu_custom_call" | custom-call | tf_op jit(solution)/shard_map/exchange/pallas_call | solution.py:521
  42.0 2.1 %finish.1 = (bf16[128,768]{1,0:T(8,128)(2,1)}, bf16[128,768]{1,0:T(8,128)(2,1)}, bf16[128,768]{1,0:T(8,128)(2,1)}, bf16[30,768]{1,0:T(8,128)(2,1)}, bf16[30,768]...) custom-call(bf16[12,64,128]{2,1,0:T(8,128)(2,1)} %get-tuple-element.11.dq, ...), custom_call_target="tpu_custom_call" | custom-call | tf_op jit(solution)/shard_map/finish/pallas_call | solution.py:593

commit v3 on v2

--- a/solution.py
+++ b/solution.py
@@ -94,6 +94,7 @@
     zc_rs,
     xy_ss,
     xy_rs,
+    round_sem,
 ):
     rows = query_hbm.shape[0]
     half_rows = half_key_hbm.shape[0]
@@ -152,7 +153,10 @@
         device(x, (z + d) % n_z, y, (core + p) % 2) for d in range(n_z) for p in range(2)
     ][1:]
     xy_peers = [device((x + d) % n_x, z, chip(dy), core) for d in range(n_x) for dy in range(CHIPS)][1:]
-    partners = [(seq, 1 - head)] + [(peer, head) for peer in zc_peers + xy_peers]
+    near_peers = [sibling] + [device(x, z, chip(dy), core) for dy in range(1, CHIPS)]
+    near_peers += [device((x + d) % n_x, z, y, core) for d in (1, n_x - 1)]
+    near_peers += [device(x, (z + d) % n_z, y, core) for d in (1, n_z - 1)]
+    partners = [(seq, 1 - head)] + [(peer, head) for peer in near_peers]
     barrier = pltpu.get_barrier_semaphore()
     for seq_to, head_to in partners:
         pl.semaphore_signal(
@@ -186,6 +190,15 @@
         c.start()
         z_copies.append(c)
     qa_copies = {}
+
+    def greet(i):
+        for peer in near_peers:
+            pl.semaphore_signal(
+                round_sem.at[i], inc=1, device_id={"seq": peer, "head": head}, device_id_type=MESH
+            )
+
+    def greeted(i):
+        pl.semaphore_wait(round_sem.at[i], len(near_peers))
 
     def send_tile(t):
         for dy in (1, 3, 2):
@@ -221,6 +234,7 @@
         sib_copies.append(c)
         kv_all[j, 0, 0] = kv_send[HEADS * y + j]
 
+    greet(0)
     loads[7].wait()
     loads[8].wait()
     row_id = lax.broadcasted_iota(jnp.int32, (rows, LANES), 0)
@@ -249,7 +263,6 @@
             fwd_copies[j, dy] = c
 
     forward(0)
-    forward(1)
     for i in range(FAR):
         z_copies[i].wait_recv()
         at = pl.multiple_of((1 - head) * width + i * far_cols, LANES)
@@ -265,7 +278,6 @@
     for c in range(CHIPS):
         qa_send[HEADS * c + 2] = joined(query, HEADS * c + 2, adjoint, HEADS * c + 2)
     send_tile(2)
-    forward(2)
 
     bias_row = lax.broadcasted_iota(jnp.int32, (8, LANES), 0)
     bias_lane = lax.broadcasted_iota(jnp.int32, (8, LANES), 1)
@@ -375,11 +387,12 @@
         c = pltpu.make_async_copy(dq_send.at[j, 0], dq_out.at[my_head], dq_ss.at[j, 0])
         c.start()
         own_copies.append(c)
-        part_send[j] = dot(low[j, near:], both, 1, 0).astype(BF)
+        grads = dot(both, low[j], 0, 1).T
+        part_send[j] = grads[near:].astype(BF)
         c = copy(part_send.at[j], part_got.at[j], part_ss.at[j], part_rs.at[j], sibling)
         c.start()
         part_copies[j] = c
-        own_sum[j] = dot(low[j, :near], both, 1, 0)
+        own_sum[j] = grads[:near]
 
     def send_keys(j):
         my_head = HEADS * y + j
@@ -420,11 +433,15 @@
             total = total + slots[i]
         return total
 
+    greeted(0)
+    greet(1)
     wait_tile(0)
     wait_keys(0)
     score_pass(0)
+    forward(1)
     wait_keys(1)
     score_pass(1)
+    forward(2)
     wait_tile(1)
     bias_total = dscore_pass(0)
     products(0)
@@ -434,6 +451,7 @@
     wait_tile(2)
     score_pass(2)
     bias_total = bias_total + dscore_pass(2)
+    greeted(1)
     zc_copies = spread(bias_total, 0, zc_peers, bias_zc, 2 * z + core, zc_ss, zc_rs)
     products(1)
     products(2)
@@ -571,6 +589,7 @@
             dma((2 * n_z,)),
             dma((n_x * CHIPS,)),
             dma((n_x * CHIPS,)),
+            pltpu.SemaphoreType.REGULAR((2,)),
         ],
         compiler_params=pltpu.CompilerParams(
             collective_id=0, has_side_effects=True, vmem_limit_bytes=62 << 20

time: 44.2 us -> 41.8 us (0.946)
  Pallas kernels: 43.5 us -> 41 us
    pallas_call x1, Pallas kernels: 41.3 us -> 38.9 us  [shards(): pl.pallas_call(functools.partial(exchange_kernel, n_x, n_z), out_shape=(j...]
where the time goes in v3:
time: 41.8 us; the launch traced here: 41.7 us
  Pallas kernels  41 us (98%)
  between operations  0.65 us (2%)
    pallas_call x1, Pallas kernels, shards(): pl.pallas_call(functools.partial(exchange_kernel, n_x, n_z), out_shape=(j...  38.9 us
    pallas_call x1, Pallas kernels, shards(): pl.pallas_call(functools.partial(finish_kernel, half_rows, quart_rows), o...  2.13 us

profile of v3, /device:TPU:1, one launch (start us, length us, event | category | flops | bytes accessed | tf_op | source)
XLA Modules:
  0.0 41.7 jit_solution(16809599226983542258)
XLA Ops:
  0.6 38.9 %exchange.1 = (bf16[12,64,128]{2,1,0:T(8,128)(2,1)}, bf16[12,176,128]{2,1,0:T(8,128)(2,1)}, f32[8,128]{1,0:T(8,128)}) custom-call(bf16[128,768]{1,0:T(8,128)(2,1)} %query_hbm.1, bf16[128,768]{1,0:T(8,128)(2,1)} %key_hbm.1, bf16[128,768]{1,0:T(8,128)(2,1)} %value_hbm.1, bf16[128,768]{1,0:T(8,128)(2,1)} %grad_hbm.1, bf16[1536,768]{1,0:T(8,128)(2,1)} %weight_hbm.1, ...), custom_call_target="tpu_custom_call" | custom-call | tf_op jit(solution)/shard_map/exchange/pallas_call | solution.py:539
  39.5 2.1 %finish.1 = (bf16[128,768]{1,0:T(8,128)(2,1)}, bf16[128,768]{1,0:T(8,128)(2,1)}, bf16[128,768]{1,0:T(8,128)(2,1)}, bf16[30,768]{1,0:T(8,128)(2,1)}, bf16[30,768]...) custom-call(bf16[12,64,128]{2,1,0:T(8,128)(2,1)} %get-tuple-element.11.dq, ...), custom_call_target="tpu_custom_call" | custom-call | tf_op jit(solution)/shard_map/finish/pallas_call | solution.py:612

commit v4 on v3

--- a/solution.py
+++ b/solution.py
@@ -201,7 +201,7 @@
         pl.semaphore_wait(round_sem.at[i], len(near_peers))
 
     def send_tile(t):
-        for dy in (1, 3, 2):
+        for dy in (2, 1, 3):
             c = copy(
                 qa_send.at[HEADS * chip(dy) + t],
                 qa_all.at[t, dy],
@@ -217,7 +217,7 @@
     kv_copies = {}
     sib_copies = []
     for j in range(HEADS):
-        for dy in (1, 3, 2):
+        for dy in (2, 1, 3):
             c = copy(
                 kv_send.at[HEADS * chip(dy) + j],
                 kv_all.at[j, 0, dy],
@@ -250,7 +250,7 @@
     fwd_copies = {}
 
     def forward(j):
-        for dy in (1, 3, 2):
+        for dy in (2, 1, 3):
             kv_copies[j, dy].wait_recv()
             c = copy(
                 kv_all.at[j, 0, dy],
@@ -293,11 +293,11 @@
         return total
 
     def wait_tile(t):
-        for dy in (1, 3, 2):
+        for dy in (2, 1, 3):
             qa_copies[t, dy].wait_recv()
 
     def wait_keys(j):
-        for dy in (1, 3, 2):
+        for dy in (2, 1, 3):
             fwd_copies[j, dy].wait_recv()
         sib_copies[j].wait_recv()
 
@@ -374,7 +374,7 @@
         dq = (dot(kv, low[j, :, :queries], 0, 0)[at : at + HD] * F32(HD**-0.5)).astype(BF)
         for dy in range(CHIPS):
             dq_send[j, dy] = dq[:, dy * rows : (dy + 1) * rows]
-        for dy in (1, 3, 2):
+        for dy in (2, 1, 3):
             c = copy(
                 dq_send.at[j, dy],
                 dq_out.at[my_head],
@@ -397,7 +397,7 @@
     def send_keys(j):
         my_head = HEADS * y + j
         part_copies[j].wait()
-        for dy in (1, 3, 2, 0):
+        for dy in (2, 1, 3, 0):
             at = slice(dy * block, (dy + 1) * block)
             dkv_send[j, dy] = (own_sum[j, at] + part_got[j, at].astype(F32)).astype(BF)
             if dy == 0:

time: 41.8 us -> 41.4 us (level)
  no operation moved by 1% of the time
where the time goes in v4:
time: 41.4 us; the launch traced here: 41.3 us
  Pallas kernels  40.7 us (98%)
  between operations  0.65 us (2%)
    pallas_call x1, Pallas kernels, shards(): pl.pallas_call(functools.partial(exchange_kernel, n_x, n_z), out_shape=(j...  38.5 us
    pallas_call x1, Pallas kernels, shards(): pl.pallas_call(functools.partial(finish_kernel, half_rows, quart_rows), o...  2.13 us

profile of v4, /device:TPU:1, one launch (start us, length us, event | category | flops | bytes accessed | tf_op | source)
XLA Modules:
  0.0 41.3 jit_solution(18107091847557970839)
XLA Ops:
  0.6 38.5 %exchange.1 = (bf16[12,64,128]{2,1,0:T(8,128)(2,1)}, bf16[12,176,128]{2,1,0:T(8,128)(2,1)}, f32[8,128]{1,0:T(8,128)}) custom-call(bf16[128,768]{1,0:T(8,128)(2,1)} %query_hbm.1, bf16[128,768]{1,0:T(8,128)(2,1)} %key_hbm.1, bf16[128,768]{1,0:T(8,128)(2,1)} %value_hbm.1, bf16[128,768]{1,0:T(8,128)(2,1)} %grad_hbm.1, bf16[1536,768]{1,0:T(8,128)(2,1)} %weight_hbm.1, ...), custom_call_target="tpu_custom_call" | custom-call | tf_op jit(solution)/shard_map/exchange/pallas_call | solution.py:539
  39.2 2.1 %finish.1 = (bf16[128,768]{1,0:T(8,128)(2,1)}, bf16[128,768]{1,0:T(8,128)(2,1)}, bf16[128,768]{1,0:T(8,128)(2,1)}, bf16[30,768]{1,0:T(8,128)(2,1)}, bf16[30,768]...) custom-call(bf16[12,64,128]{2,1,0:T(8,128)(2,1)} %get-tuple-element.11.dq, ...), custom_call_target="tpu_custom_call" | custom-call | tf_op jit(solution)/shard_map/finish/pallas_call | solution.py:612

commit v5 on v4

--- a/solution.py
+++ b/solution.py
@@ -621,8 +621,18 @@
             like(quart_value),
             like(section_bias),
         ),
-        in_specs=[vmem] * 3,
-        out_specs=(vmem,) * 8,
+        grid=(2,),
+        in_specs=[
+            pl.BlockSpec((heads // 2, HD, rows), lambda i: (i, 0, 0)),
+            pl.BlockSpec((heads // 2, block, LANES), lambda i: (i, 0, 0)),
+            pl.BlockSpec((8, LANES), lambda i: (0, 0)),
+        ],
+        out_specs=(
+            *[pl.BlockSpec((n, width // 2), lambda i: (0, i)) for n in [rows] * 3],
+            *[pl.BlockSpec((half_rows, width // 2), lambda i: (0, i))] * 2,
+            *[pl.BlockSpec((quart_rows, width // 2), lambda i: (0, i))] * 2,
+            pl.BlockSpec(section_bias.shape, lambda i: (0, 0)),
+        ),
         compiler_params=pltpu.CompilerParams(vmem_limit_bytes=62 << 20),
         name="finish",
     )(dq, dkv, bias)

time: 41.4 us -> 41.4 us (level)
  no operation moved by 1% of the time
where the time goes in v5:
time: 41.4 us; the launch traced here: 41.3 us
  Pallas kernels  40.6 us (98%)
  between operations  0.65 us (2%)
    pallas_call x1, Pallas kernels, shards(): pl.pallas_call(functools.partial(exchange_kernel, n_x, n_z), out_shape=(j...  38.5 us
    pallas_call x1, Pallas kernels, shards(): pl.pallas_call(functools.partial(finish_kernel, half_rows, quart_rows), o...  2.09 us

profile of v5, /device:TPU:1, one launch (start us, length us, event | category | flops | bytes accessed | tf_op | source)
XLA Modules:
  0.0 41.3 jit_solution(9611755510027138616)
XLA Ops:
  0.6 38.5 %exchange.1 = (bf16[12,64,128]{2,1,0:T(8,128)(2,1)}, bf16[12,176,128]{2,1,0:T(8,128)(2,1)}, f32[8,128]{1,0:T(8,128)}) custom-call(bf16[128,768]{1,0:T(8,128)(2,1)} %query_hbm.1, bf16[128,768]{1,0:T(8,128)(2,1)} %key_hbm.1, bf16[128,768]{1,0:T(8,128)(2,1)} %value_hbm.1, bf16[128,768]{1,0:T(8,128)(2,1)} %grad_hbm.1, bf16[1536,768]{1,0:T(8,128)(2,1)} %weight_hbm.1, ...), custom_call_target="tpu_custom_call" | custom-call | tf_op jit(solution)/shard_map/exchange/pallas_call | solution.py:539
  39.2 2.1 %finish.1 = (bf16[128,768]{1,0:T(8,128)(2,1)}, bf16[128,768]{1,0:T(8,128)(2,1)}, bf16[128,768]{1,0:T(8,128)(2,1)}, bf16[30,768]{1,0:T(8,128)(2,1)}, bf16[30,768]...) custom-call(bf16[12,64,128]{2,1,0:T(8,128)(2,1)} %get-tuple-element.11.dq, ...), custom_call_target="tpu_custom_call" | custom-call | tf_op jit(solution)/shard_map/finish/pallas_call | solution.py:612
